TPU v7x, 32 devices: a whole 2x2x4 slice. The times are simulated.
32 devices in a mesh: groups: 2 (over x), seq: 16 (over z, y, core).
Axes of the slice: x: 2, y: 2, z: 4, core: 2. Of those that a mesh axis runs over, the one named last changes fastest.
Arguments:
- queries: bfloat16 [12288, 2048], P(('groups', 'seq')), parts along dimension 0, may hold values from -6 to 6
- keys: bfloat16 [12288, 2048], P(('groups', 'seq')), parts along dimension 0, may hold values from -6 to 6
- values: bfloat16 [12288, 2048], P(('groups', 'seq')), parts along dimension 0, may hold values from -6 to 6
- out_grad: bfloat16 [12288, 2048], P(('groups', 'seq')), parts along dimension 0, may hold values from -6 to 6
Outputs:
- relaid: bfloat16 [16, 12288, 128], P('seq', 'groups'), parts along dimension 1
- query_grad: bfloat16 [12288, 2048], P(('groups', 'seq')), parts along dimension 0
- key_grad: bfloat16 [12288, 2048], P(('groups', 'seq')), parts along dimension 0
- value_grad: bfloat16 [12288, 2048], P(('groups', 'seq')), parts along dimension 0
There are 2 independent parts, one for each index of `groups`. A program takes and returns all parts, laid end to end along the dimension named above; each array names one. Nothing has to cross between parts.
All inputs are finite; a program needn't handle non-finite values.
Results may differ from a plain program's by a relative error of at most 0.0058.
Values may be sent and summed in bfloat16 or wider, within the bound.
A program may use at most 128 MiB of HBM per device.

v0:
```python
import jax
import jax.numpy as jnp
from jax import lax
from jax.sharding import PartitionSpec as P

DH = 128
eps = 1e-06


def blocks_before(columns, earlier):
    count = columns.shape[0]
    row_ids = lax.broadcasted_iota(jnp.int32, (count, count), 0)
    col_ids = lax.broadcasted_iota(jnp.int32, (count, count), 1)
    if earlier:
        select = (col_ids < row_ids).astype(jnp.float32)
    else:
        select = (col_ids > row_ids).astype(jnp.float32)
    summed = jnp.dot(
        select, columns, precision=lax.Precision.HIGHEST, preferred_element_type=jnp.float32
    )
    return summed


def earlier_sum(local):
    flat = local.reshape(1, -1)
    columns = lax.all_to_all(flat, "seq", split_axis=1, concat_axis=0, tiled=True)
    shifted = blocks_before(columns, True)
    merged = lax.all_to_all(
        shifted.astype(jnp.bfloat16), "seq", split_axis=0, concat_axis=1, tiled=True
    ).astype(shifted.dtype)
    return merged.reshape(local.shape)


def later_sum(local):
    flat = local.reshape(1, -1)
    columns = lax.all_to_all(flat, "seq", split_axis=1, concat_axis=0, tiled=True)
    shifted = blocks_before(columns, False)
    merged = lax.all_to_all(
        shifted.astype(jnp.bfloat16), "seq", split_axis=0, concat_axis=1, tiled=True
    ).astype(shifted.dtype)
    return merged.reshape(local.shape)


def body(queries, keys, values, out_grad):
    rows = queries.shape[0]
    width = queries.shape[1]
    heads = width // DH
    f32 = jnp.float32
    q3 = queries.reshape(rows, heads, DH)
    k3 = keys.reshape(rows, heads, DH)
    v3 = values.reshape(rows, heads, DH)
    row_ids = lax.broadcasted_iota(jnp.int32, (rows, rows), 0)
    col_ids = lax.broadcasted_iota(jnp.int32, (rows, rows), 1)
    causal = (row_ids >= col_ids)[None]
    local_state = jnp.einsum("shd,she->hde", k3, v3, preferred_element_type=f32)
    scores = jnp.einsum("thd,shd->hts", q3, k3, preferred_element_type=f32)
    masked = jnp.where(causal, scores, 0.0).astype(jnp.bfloat16)
    intra = jnp.einsum("hts,shd->thd", masked, v3, preferred_element_type=f32)
    prefix_b = earlier_sum(local_state).astype(jnp.bfloat16)
    inter = jnp.einsum("thd,hde->the", q3, prefix_b, preferred_element_type=f32)
    acc = intra + inter
    norm = jnp.sqrt(jnp.mean(acc * acc, axis=-1, keepdims=True) + eps)
    unit = acc / norm
    out_heads = unit.astype(jnp.bfloat16)
    splits = lax.axis_size("seq") // heads
    piece_rows = rows // splits
    outgoing = out_heads.reshape(splits, piece_rows, heads, DH)
    outgoing = jnp.transpose(outgoing, (0, 2, 1, 3)).reshape(splits * heads, piece_rows, DH)
    relaid = lax.all_to_all(outgoing, "seq", split_axis=0, concat_axis=1, tiled=True)
    grad_rows = out_grad.reshape(rows, heads, DH).astype(f32)
    inner = jnp.mean(grad_rows * unit, axis=-1, keepdims=True)
    d_acc = ((grad_rows - unit * inner) / norm).astype(jnp.bfloat16)
    back_state = jnp.einsum("thd,the->hde", q3, d_acc, preferred_element_type=f32)
    later_b = later_sum(back_state).astype(jnp.bfloat16)
    dscore = jnp.einsum("thd,shd->hts", d_acc, v3, preferred_element_type=f32)
    dscore = jnp.where(causal, dscore, 0.0).astype(jnp.bfloat16)
    query_grad = jnp.einsum("hts,shd->thd", dscore, k3, preferred_element_type=f32)
    query_grad = query_grad + jnp.einsum(
        "the,hde->thd", d_acc, prefix_b, preferred_element_type=f32
    )
    key_grad = jnp.einsum("hts,thd->shd", dscore, q3, preferred_element_type=f32)
    key_grad = key_grad + jnp.einsum("she,hde->shd", v3, later_b, preferred_element_type=f32)
    value_grad = jnp.einsum("hts,the->she", masked, d_acc, preferred_element_type=f32)
    value_grad = value_grad + jnp.einsum("shd,hde->she", k3, later_b, preferred_element_type=f32)
    return (
        relaid,
        query_grad.astype(jnp.bfloat16).reshape(rows, width),
        key_grad.astype(jnp.bfloat16).reshape(rows, width),
        value_grad.astype(jnp.bfloat16).reshape(rows, width),
    )


def solution(mesh):
    return jax.shard_map(
        body,
        mesh=mesh,
        in_specs=(
            P(("groups", "seq"), None),
            P(("groups", "seq"), None),
            P(("groups", "seq"), None),
            P(("groups", "seq"), None),
        ),
        out_specs=(
            P("seq", "groups", None),
            P(("groups", "seq"), None),
            P(("groups", "seq"), None),
            P(("groups", "seq"), None),
        ),
        check_vma=False,
    )
```

profile of v0, /device:TPU:0, one launch (start us, length us, event | category | flops | bytes accessed | tf_op | source)
XLA Modules:
  0.0 182.9 jit_solution(17124694191122851817)
XLA Ops:
  0.6 0.0 copy-start
  0.6 3.1 %copy.111 = bf16[48,8,16,128]{3,2,1,0:T(8,128)(2,1)} copy(bf16[48,8,16,128]{3,1,2,0:T(8,128)(2,1)} %bitcast.126) | data formatting | bytes 3145728
  3.7 2.1 %copy.79 = bf16[384,16,128]{0,2,1:T(8,128)(2,1)S(1)} copy(bf16[384,16,128]{2,1,0:T(8,128)(2,1)} %bitcast.125) | data formatting | bytes 3145728 | tf_op jit(solution)/shard_map/reshape | solution.py:50
  5.9 0.0 copy-done
  5.9 0.0 copy-start.4
  5.9 0.6 fusion.8
  6.5 0.6 copy-done.4
  7.0 32.0 %all_to_all.76 = f32[1,16,16384]{2,0,1:T(1,128)S(1)} all-to-all(f32[1,16,16384]{2,0,1:T(1,128)S(1)} %bitcast.135), channel_id=1, replica_groups=mesh['groups'=2,'seq'=16] {'seq'}, dimensions={1} | all-to-all | bytes 2097152 | tf_op jit(solution)/shard_map/all_to_all | solution.py:26
  39.0 1.2 fusion
  40.2 0.5 broadcast.25
  40.8 0.9 reduce.2
  41.7 1.2 reshape.106
  42.9 5.1 %all-to-all-start.1 = ((bf16[16,2,8192]{2,1,0:T(2,128)(2,1)}), bf16[16,2,8192]{2,1,0:T(2,128)(2,1)}, u32[]{:S(2)}, u32[]{:S(2)}) async-start(bf16[16,2,8192]{2,1,0:T(2,128)(2,1)} %reshape.106), calls=%async_computation.1 | async-start | bytes 1048576 | tf_op jit(solution)/shard_map/all_to_all | solution.py:28
  48.0 0.0 copy-start.6
  48.0 3.2 %copy.86 = f32[384,2048]{0,1:T(8,128)} copy(bf16[384,2048]{1,0:T(8,128)(2,1)} %param.7) | data formatting | bytes 4718592 | tf_op jit(solution)/shard_map/convert_element_type | solution.py:70
  51.2 0.0 copy-done.6
  51.2 4.9 %select_convert_fusion.1 = bf16[16,384,384]{2,1,0:T(8,128)(2,1)} fusion(pred[384,384]{1,0:T(8,128)(4,1)S(1)} %iota_compare_fusion, bf16[384,2048]{1,0:T(8,128)(2,1)} %param.5, bf16[384,2048]{1,0:T(8,128)(2,1)S(1)} %copy-done.6), kind=kOutput, calls=%fused_computation.5 | convolution fusion | flops 608698368 | bytes 8011776 | tf_op jit(solution)/shard_map/thd,shd->hts/dot_general | solution.py:56
  56.2 6.3 %all-to-all-done.1 = bf16[16,2,8192]{2,1,0:T(2,128)(2,1)} async-done(((bf16[16,2,8192]{2,1,0:T(2,128)(2,1)}), bf16[16,2,8192]{2,1,0:T(2,128)(2,1)}, u32[]{:S(2)}, u32[]{:S(2)}) %all-to-all-start.1) | async-done | bytes 524320 | tf_op jit(solution)/shard_map/all_to_all | solution.py:28
  62.5 3.5 %reshape.107 = bf16[16,1,16384]{2,1,0:T(2,128)(2,1)} reshape(bf16[16,2,8192]{2,1,0:T(2,128)(2,1)} %all-to-all-done.1) | data formatting | bytes 1048576
  65.9 5.1 %reduce = bf16[16,16384]{1,0:T(8,128)(2,1)} reduce(bf16[16,1,16384]{2,1,0:T(2,128)(2,1)} %reshape.107, bf16[]{:T(256)} %constant.8), dimensions={1}, to_apply=%all_to_all.61.reduce_sub_computation | reduce | bytes 1048578 | tf_op jit(solution)/shard_map/all_to_all | solution.py:28
  71.0 1.1 copy.112
  72.1 0.0 copy-start.10
  72.2 0.0 copy-start.2
  72.2 0.8 fusion.16
  73.0 0.0 copy-done.10
  73.0 1.7 copy-done.2
  74.7 1.6 multiply_reduce_fusion.1
  76.3 0.3 copy-done.1
  76.6 0.6 multiply_reduce_fusion
  77.2 0.0 copy-start.7
  77.2 2.0 %divide_convert_fusion = (bf16[384,16,128]{0,2,1:T(8,128)(2,1)S(1)}, bf16[16,384,128]{1,2,0:T(8,128)(2,1)}) fusion(f32[384,16]{0,1:T(8,128)S(1)} %broadcast_multiply_fusion, f32[384,16]{0,1:T(8,128)S(1)} %add_sqrt_fusion, f32[384,2048]{0,1:T(8,128)S(1)} %copy-done.1, f32[384,16,128]{0,2,1:T(8,128)S(1)} %get-tuple-element.23), kind=kLoop, calls=%fused_computation.12 | loop fusion | flops 4718592 | bytes 9486336 | tf_op jit(solution)/shard_map/convert_element_type | solution.py:72
  79.2 0.0 copy-done.7
  79.2 1.6 fusion.20
  80.8 2.5 %copy.93 = f32[16,128,128]{2,1,0:T(8,128)} copy(f32[16,128,128]{1,2,0:T(8,128)} %fusion.20) | data formatting | bytes 2097152 | tf_op jit(solution)/shard_map/thd,the->hde/dot_general | solution.py:73
  83.3 28.9 %all_to_all.77 = f32[1,16,16384]{2,0,1:T(1,128)S(1)} all-to-all(f32[1,16,16384]{2,0,1:T(1,128)} %bitcast.134), channel_id=1, replica_groups=mesh['groups'=2,'seq'=16] {'seq'}, dimensions={1} | all-to-all | bytes 2097152 | tf_op jit(solution)/shard_map/all_to_all | solution.py:36
  112.2 2.0 %fusion.1 = bf16[16,1,16384]{2,0,1:T(8,128)(2,1)} fusion(f32[1,16,16384]{2,0,1:T(1,128)S(1)} %all_to_all.77), kind=kOutput, calls=%fused_computation.3 | convolution fusion | flops 50594048 | bytes 1572864 | tf_op jit(solution)/shard_map/dot_general | solution.py:18
  114.2 2.6 %reduce.3 = bf16[16,16384]{1,0:T(8,128)(2,1)} reduce(bf16[16,1,16384]{2,0,1:T(8,128)(2,1)} %fusion.1, bf16[]{:T(256)} %broadcast.25), dimensions={1}, to_apply=%copy.95.reduce_sub_computation | reduce | bytes 1048578 | tf_op jit(solution)/shard_map/all_to_all | solution.py:38
  116.9 2.2 %reshape.108 = bf16[16,2,8192]{2,1,0:T(2,128)(2,1)} reshape(bf16[16,16384]{1,0:T(8,128)(2,1)} %reduce.3) | data formatting | bytes 1048576
  119.1 19.6 %all_to_all.78 = bf16[16,2,8192]{2,1,0:T(2,128)(2,1)} all-to-all(bf16[16,2,8192]{2,1,0:T(2,128)(2,1)} %reshape.108), channel_id=1, replica_groups=mesh['groups'=2,'seq'=16] {'seq'}, dimensions={0} | all-to-all | bytes 1048576 | tf_op jit(solution)/shard_map/all_to_all | solution.py:38
  138.7 4.6 %all-to-all-start.2 = ((bf16[16,384,128]{1,2,0:T(8,128)(2,1)}), bf16[16,384,128]{1,2,0:T(8,128)(2,1)}, u32[]{:S(2)}, u32[]{:S(2)}) async-start(bf16[16,384,128]{1,2,0:T(8,128)(2,1)} %get-tuple-element.21), calls=%async_computation.2 | async-start | bytes 3145728 | tf_op jit(solution)/shard_map/all_to_all | solution.py:69
  143.3 1.6 fusion.35
  144.9 0.0 copy-start.5
  144.9 1.7 select_convert_fusion
  146.6 0.0 copy-done.5
  146.6 0.0 copy-start.3
  146.6 2.7 %fusion.3 = bf16[384,16,128]{0,2,1:T(8,128)(2,1)} fusion(f32[16,128,384]{2,1,0:T(8,128)S(1)} %fusion.35, bf16[16,384,384]{2,1,0:T(8,128)(2,1)S(1)} %select_convert_fusion, bf16[384,16,128]{0,2,1:T(8,128)(2,1)S(1)} %copy-done.5), kind=kOutput, calls=%fused_computation.9 | convolution fusion | flops 605552640 | bytes 11010048 | tf_op jit(solution)/shard_map/hts,shd->thd/dot_general | solution.py:77
  149.3 0.0 copy-done.3
  149.3 2.6 %copy.99 = bf16[384,2048]{1,0:T(8,128)(2,1)} copy(bf16[384,2048]{0,1:T(8,128)(2,1)} %bitcast.127) | data formatting | bytes 3145728
  151.9 5.2 %fusion.36 = f32[16,128,384]{2,1,0:T(8,128)} fusion(bf16[384,16,128]{0,2,1:T(8,128)(2,1)S(1)} %get-tuple-element.20, bf16[16,384,384]{2,1,0:T(8,128)(2,1)} %select_convert_fusion.1), kind=kOutput, calls=%fused_computation.52 | convolution fusion | flops 603979776 | bytes 9437184 | tf_op jit(solution)/shard_map/hts,the->she/dot_general | solution.py:83
  157.1 3.5 %reshape.109 = bf16[16,1,16384]{2,1,0:T(2,128)(2,1)} reshape(bf16[16,2,8192]{2,1,0:T(2,128)(2,1)} %all_to_all.78) | data formatting | bytes 1048576
  160.6 5.2 %reduce.1 = bf16[16,16384]{1,0:T(8,128)(2,1)} reduce(bf16[16,1,16384]{2,1,0:T(2,128)(2,1)} %reshape.109, bf16[]{:T(256)} %constant.8), dimensions={1}, to_apply=%all_to_all.69.reduce_sub_computation | reduce | bytes 1048578 | tf_op jit(solution)/shard_map/all_to_all | solution.py:38
  165.8 1.1 copy.113
  166.9 0.0 copy-start.11
  166.9 0.0 copy-done.9
  166.9 4.0 %add_convert_fusion = bf16[16,128,384]{2,1,0:T(8,128)(2,1)} fusion(f32[16,128,384]{2,1,0:T(8,128)} %fusion.36, bf16[16,128,128]{2,1,0:T(8,128)(2,1)S(1)} %bitcast.132, bf16[384,2048]{1,0:T(8,128)(2,1)S(1)} %copy-done.9), kind=kOutput, calls=%fused_computation.11 | convolution fusion | flops 202899456 | bytes 6815744 | tf_op jit(solution)/shard_map/shd,hde->she/dot_general | solution.py:84
  170.9 0.0 copy-done.11
  170.9 2.6 %copy.101 = bf16[384,2048]{1,0:T(8,128)(2,1)} copy(bf16[384,2048]{0,1:T(8,128)(2,1)} %bitcast.129) | data formatting | bytes 3145728
  173.6 0.0 copy-done.12
  173.6 0.8 fusion.5
  174.4 0.6 copy-done.8
  175.0 3.7 %fusion.2 = bf16[384,16,128]{0,2,1:T(8,128)(2,1)S(1)} fusion(f32[16,128,384]{2,1,0:T(8,128)S(1)} %fusion.5, bf16[16,384,384]{2,1,0:T(8,128)(2,1)} %copy-done.3, bf16[384,2048]{1,0:T(8,128)(2,1)S(1)} %copy-done.8), kind=kOutput, calls=%fused_computation.7 | convolution fusion | flops 605552640 | bytes 11010048 | tf_op jit(solution)/shard_map/hts,thd->shd/dot_general | solution.py:81
  178.7 1.6 copy.100
  180.3 0.0 all-to-all-done.2
  180.3 2.6 %copy.85 = bf16[16,384,128]{2,1,0:T(8,128)(2,1)} copy(bf16[16,384,128]{1,2,0:T(8,128)(2,1)} %all-to-all-done.2) | data formatting | bytes 3145728 | tf_op jit(solution)/shard_map/all_to_all | solution.py:69
  (7 shorter events, 0.1 us)
Async XLA Ops:
  0.6 5.2 %copy-start = (bf16[384,2048]{1,0:T(8,128)(2,1)S(1)}, bf16[384,2048]{1,0:T(8,128)(2,1)}, u32[]{:S(2)}) copy-start(bf16[384,2048]{1,0:T(8,128)(2,1)} %param.6) | copy-start | bytes 4718596
  5.9 1.1 copy-start.4
  42.9 19.6 %all-to-all-start.1 = ((bf16[16,2,8192]{2,1,0:T(2,128)(2,1)}), bf16[16,2,8192]{2,1,0:T(2,128)(2,1)}, u32[]{:S(2)}, u32[]{:S(2)}) async-start(bf16[16,2,8192]{2,1,0:T(2,128)(2,1)} %reshape.106), calls=%async_computation.1 | async-start | bytes 1048576 | tf_op jit(solution)/shard_map/all_to_all | solution.py:28
  48.0 3.3 %copy-start.6 = (bf16[384,2048]{1,0:T(8,128)(2,1)S(1)}, bf16[384,2048]{1,0:T(8,128)(2,1)}, u32[]{:S(2)}) copy-start(bf16[384,2048]{1,0:T(8,128)(2,1)} %param.4) | copy-start | bytes 4718596
  72.1 0.8 copy-start.10
  72.2 2.5 %copy-start.2 = (bf16[16,384,384]{2,1,0:T(8,128)(2,1)S(1)}, bf16[16,384,384]{2,1,0:T(8,128)(2,1)}, u32[]{:S(2)}) copy-start(bf16[16,384,384]{2,1,0:T(8,128)(2,1)} %select_convert_fusion.1) | copy-start | bytes 14155780
  74.7 1.9 %copy-start.1 = (f32[384,2048]{0,1:T(8,128)S(1)}, f32[384,2048]{0,1:T(8,128)}, u32[]{:S(2)}) copy-start(f32[384,2048]{0,1:T(8,128)} %copy.86) | copy-start | bytes 9437188
  77.2 2.0 %copy-start.7 = (bf16[384,2048]{1,0:T(8,128)(2,1)S(1)}, bf16[384,2048]{1,0:T(8,128)(2,1)}, u32[]{:S(2)}) copy-start(bf16[384,2048]{1,0:T(8,128)(2,1)} %param.4) | copy-start | bytes 4718596
  138.7 41.7 %all-to-all-start.2 = ((bf16[16,384,128]{1,2,0:T(8,128)(2,1)}), bf16[16,384,128]{1,2,0:T(8,128)(2,1)}, u32[]{:S(2)}, u32[]{:S(2)}) async-start(bf16[16,384,128]{1,2,0:T(8,128)(2,1)} %get-tuple-element.21), calls=%async_computation.2 | async-start | bytes 3145728 | tf_op jit(solution)/shard_map/all_to_all | solution.py:69
  144.9 1.7 copy-start.5
  146.6 2.7 %copy-start.3 = (bf16[16,384,384]{2,1,0:T(8,128)(2,1)}, bf16[16,384,384]{2,1,0:T(8,128)(2,1)S(1)}, u32[]{:S(2)}) copy-start(bf16[16,384,384]{2,1,0:T(8,128)(2,1)S(1)} %select_convert_fusion) | copy-start | bytes 14155780
  160.6 6.3 %copy-start.9 = (bf16[384,2048]{1,0:T(8,128)(2,1)S(1)}, bf16[384,2048]{1,0:T(8,128)(2,1)}, u32[]{:S(2)}) copy-start(bf16[384,2048]{1,0:T(8,128)(2,1)} %param.5) | copy-start | bytes 4718596
  166.9 4.1 %copy-start.11 = (bf16[2,8,128,128]{3,2,1,0:T(8,128)(2,1)}, bf16[2,8,128,128]{3,2,1,0:T(8,128)(2,1)S(1)}, u32[]{:S(2)}) copy-start(bf16[2,8,128,128]{3,2,1,0:T(8,128)(2,1)S(1)} %copy.113) | copy-start | bytes 1572868
  170.9 2.6 %copy-start.12 = (bf16[2,8,128,128]{3,2,1,0:T(8,128)(2,1)S(1)}, bf16[2,8,128,128]{3,2,1,0:T(8,128)(2,1)}, u32[]{:S(2)}) copy-start(bf16[2,8,128,128]{3,2,1,0:T(8,128)(2,1)} %copy-done.11) | copy-start | bytes 1572868
  173.6 1.4 copy-start.8
where the time goes:
time: 184 us; the launch traced here: 183 us
  blocking collectives  80.5 us (44%)
  local copies, waits for them, and re-layouts  36.6 us (20%)
  matrix products  32.4 us (18%)
  other arithmetic  16.5 us (9%)
  starting transfers between devices  9.68 us (5%)
  waiting for transfers between devices  6.29 us (3%)
    all_to_all x1, blocking collectives, earlier_sum(): lax.all_to_all(flat, 'seq', split_axis=1, concat_axis=0, tiled=True)  32 us
    all_to_all x1, blocking collectives, later_sum(): lax.all_to_all(flat, 'seq', split_axis=1, concat_axis=0, tiled=True)  28.9 us
    unnamed x36, local copies, waits for them, and re-layouts  25.7 us
    all_to_all x1, blocking collectives, later_sum(): lax.all_to_all(shifted.astype(jnp.bfloat16), 'seq', split_axis=0, concat_...  19.6 us
    all_to_all x2, other arithmetic, later_sum(): lax.all_to_all(shifted.astype(jnp.bfloat16), 'seq', split_axis=0, concat_...  7.82 us
    all_to_all x1, waiting for transfers between devices, earlier_sum(): lax.all_to_all(shifted.astype(jnp.bfloat16), 'seq', split_axis=0, concat_...  6.29 us
    all_to_all x2, other arithmetic, earlier_sum(): lax.all_to_all(shifted.astype(jnp.bfloat16), 'seq', split_axis=0, concat_...  6.02 us
    dot_general x1, matrix products, body(): jnp.einsum('hts,the->she', masked, d_acc, preferred_element_type=f32)  5.18 us
  transfers between devices with their start and end apart: 2, of which 1 were waited for; matrix products, arithmetic and copies ran while one was open for 24% of the time, Pallas kernels for 0%

commit v1 on v0

--- a/solution.py
+++ b/solution.py
@@ -2,9 +2,22 @@
 import jax.numpy as jnp
 from jax import lax
 from jax.sharding import PartitionSpec as P
+from jax.lax import axis_index, axis_size, ppermute
 
 DH = 128
 eps = 1e-06
+
+
+def turn_strips_all_in(slab_in, in_dim, local_x):
+    response, val2 = (slab_in.shape[:in_dim], slab_in.shape[in_dim + 1 :])
+    piece_now = slab_in.reshape(*response, local_x, -1, *val2)
+    return jnp.moveaxis(piece_now, in_dim, 0)
+
+
+def recover_classes(v0, k_dim):
+    v0 = jnp.moveaxis(v0, 0, k_dim)
+    lower = v0.shape
+    return v0.reshape(*lower[:k_dim], lower[k_dim] * lower[k_dim + 1], *lower[k_dim + 2 :])
 
 
 def blocks_before(columns, earlier):
@@ -33,7 +46,18 @@
 
 def later_sum(local):
     flat = local.reshape(1, -1)
-    columns = lax.all_to_all(flat, "seq", split_axis=1, concat_axis=0, tiled=True)
+    t_next = axis_size("seq")
+    a_now = axis_index("seq")
+    raw_out, then = (t_next, a_now)
+    seen_now = turn_strips_all_in(flat, 1, raw_out)
+    frames = [seen_now[then]]
+    for dd in range(1, raw_out):
+        h_now = seen_now[(then + dd) % raw_out]
+        tile_out = ppermute(h_now, "seq", [(q, (q + dd) % raw_out) for q in range(raw_out)])
+        frames.append(tile_out)
+    placed = jnp.stack(frames)
+    seen_now = placed[(then - jnp.arange(raw_out)) % raw_out]
+    columns = recover_classes(seen_now, 0)
     shifted = blocks_before(columns, False)
     merged = lax.all_to_all(
         shifted.astype(jnp.bfloat16), "seq", split_axis=0, concat_axis=1, tiled=True

time: 184 us -> 192 us (1.043)
  blocking collectives: 80.5 us -> 52.4 us
  starting transfers between devices: 9.68 us -> 27 us
  waiting for transfers between devices: 6.29 us -> 18.1 us
  local copies, waits for them, and re-layouts: 36.6 us -> 44 us
    all_to_all x1 -> x0, blocking collectives: 28.9 us -> none  [later_sum(): lax.all_to_all(flat, 'seq', split_axis=1, concat_axis=0, tiled=True)]
    ppermute x0 -> x15, starting transfers between devices: none -> 17.4 us  [later_sum(): ppermute(h_now, 'seq', [(q, (q + dd) % raw_out) for q in range(raw_out)])]
    ppermute x0 -> x15, waiting for transfers between devices: none -> 12 us  [later_sum(): ppermute(h_now, 'seq', [(q, (q + dd) % raw_out) for q in range(raw_out)])]
    another operation x0 -> x2, local copies, waits for them, and re-layouts: none -> 4.61 us  [the longest x1 3.2 us: later_sum(): placed = jnp.stack(frames)]
    gather x0 -> x1, local copies, waits for them, and re-layouts: none -> 1.92 us  [later_sum(): seen_now = placed[(then - jnp.arange(raw_out)) % raw_out]]
    unnamed x36 -> x56, local copies, waits for them, and re-layouts: 25.7 us -> 25.6 us
  transfers between devices with their start and end apart: 2 -> 17, of which waited for: 1 -> 7; matrix products, arithmetic and copies ran while one was open for 24% -> 24% of each run, Pallas kernels for 0% -> 0%
where the time goes in v1:
time: 192 us; the launch traced here: 190 us
  blocking collectives  52.4 us (27%)
  local copies, waits for them, and re-layouts  44 us (23%)
  matrix products  32.3 us (17%)
  starting transfers between devices  27 us (14%)
  waiting for transfers between devices  18.1 us (9%)
  other arithmetic  15.4 us (8%)
    all_to_all x1, blocking collectives, earlier_sum(): lax.all_to_all(flat, 'seq', split_axis=1, concat_axis=0, tiled=True)  32 us
    unnamed x56, local copies, waits for them, and re-layouts  25.6 us
    all_to_all x1, blocking collectives, later_sum(): lax.all_to_all(shifted.astype(jnp.bfloat16), 'seq', split_axis=0, concat_...  20.4 us
    ppermute x15, starting transfers between devices, later_sum(): ppermute(h_now, 'seq', [(q, (q + dd) % raw_out) for q in range(raw_out)])  17.4 us
    ppermute x15, waiting for transfers between devices, later_sum(): ppermute(h_now, 'seq', [(q, (q + dd) % raw_out) for q in range(raw_out)])  12 us
    all_to_all x2, other arithmetic, later_sum(): lax.all_to_all(shifted.astype(jnp.bfloat16), 'seq', split_axis=0, concat_...  6.19 us
    all_to_all x1, waiting for transfers between devices, earlier_sum(): lax.all_to_all(shifted.astype(jnp.bfloat16), 'seq', split_axis=0, concat_...  6.09 us
    all_to_all x2, other arithmetic, earlier_sum(): lax.all_to_all(shifted.astype(jnp.bfloat16), 'seq', split_axis=0, concat_...  6.08 us
  transfers between devices with their start and end apart: 17, of which 7 were waited for; matrix products, arithmetic and copies ran while one was open for 24% of the time, Pallas kernels for 0%

profile of v1, /device:TPU:0, one launch (start us, length us, event | category | flops | bytes accessed | tf_op | source)
XLA Modules:
  0.0 190.4 jit_solution(13914523631299267499)
XLA Ops:
  0.6 3.1 %copy.108 = bf16[48,8,16,128]{3,2,1,0:T(8,128)(2,1)} copy(bf16[48,8,16,128]{3,1,2,0:T(8,128)(2,1)} %bitcast.172) | data formatting | bytes 3145728
  3.7 2.1 %copy.78 = bf16[384,16,128]{0,2,1:T(8,128)(2,1)S(1)} copy(bf16[384,16,128]{2,1,0:T(8,128)(2,1)} %bitcast.171) | data formatting | bytes 3145728 | tf_op jit(solution)/shard_map/reshape | solution.py:74
  5.9 0.6 fusion.8
  6.5 0.5 copy-done.6
  7.0 32.0 %all_to_all.60 = f32[1,16,16384]{2,0,1:T(1,128)S(1)} all-to-all(f32[1,16,16384]{2,0,1:T(1,128)S(1)} %bitcast.180), channel_id=1, replica_groups=mesh['groups'=2,'seq'=16] {'seq'}, dimensions={1} | all-to-all | bytes 2097152 | tf_op jit(solution)/shard_map/all_to_all | solution.py:39
  39.0 1.2 fusion
  40.2 0.6 broadcast.109
  40.8 1.0 reduce.2
  41.8 1.2 reshape.162
  43.0 5.1 %all-to-all-start.1 = ((bf16[16,2,8192]{2,1,0:T(2,128)(2,1)}), bf16[16,2,8192]{2,1,0:T(2,128)(2,1)}, u32[]{:S(2)}, u32[]{:S(2)}) async-start(bf16[16,2,8192]{2,1,0:T(2,128)(2,1)} %reshape.162), calls=%async_computation.1 | async-start | bytes 1048576 | tf_op jit(solution)/shard_map/all_to_all | solution.py:41
  48.3 3.2 %copy.85 = f32[384,2048]{0,1:T(8,128)} copy(bf16[384,2048]{1,0:T(8,128)(2,1)} %param.7) | data formatting | bytes 4718592 | tf_op jit(solution)/shard_map/convert_element_type | solution.py:94
  51.5 5.0 %select_convert_fusion.1 = bf16[16,384,384]{2,1,0:T(8,128)(2,1)} fusion(pred[384,384]{1,0:T(8,128)(4,1)S(1)} %iota_compare_fusion, bf16[384,2048]{1,0:T(8,128)(2,1)} %param.5, bf16[384,2048]{1,0:T(8,128)(2,1)S(1)} %copy-done.8), kind=kOutput, calls=%fused_computation.6 | convolution fusion | flops 608698368 | bytes 8011776 | tf_op jit(solution)/shard_map/thd,shd->hts/dot_general | solution.py:80
  56.5 6.1 %all-to-all-done.1 = bf16[16,2,8192]{2,1,0:T(2,128)(2,1)} async-done(((bf16[16,2,8192]{2,1,0:T(2,128)(2,1)}), bf16[16,2,8192]{2,1,0:T(2,128)(2,1)}, u32[]{:S(2)}, u32[]{:S(2)}) %all-to-all-start.1) | async-done | bytes 524320 | tf_op jit(solution)/shard_map/all_to_all | solution.py:41
  62.6 3.5 %reshape.163 = bf16[16,1,16384]{2,1,0:T(2,128)(2,1)} reshape(bf16[16,2,8192]{2,1,0:T(2,128)(2,1)} %all-to-all-done.1) | data formatting | bytes 1048576
  66.1 5.1 %reduce = bf16[16,16384]{1,0:T(8,128)(2,1)} reduce(bf16[16,1,16384]{2,1,0:T(2,128)(2,1)} %reshape.163, bf16[]{:T(256)} %constant.121), dimensions={1}, to_apply=%all_to_all.49.reduce_sub_computation | reduce | bytes 1048578 | tf_op jit(solution)/shard_map/all_to_all | solution.py:41
  71.1 1.1 copy.109
  72.3 0.8 fusion.16
  73.1 1.7 copy-done.4
  74.8 1.6 multiply_reduce_fusion.1
  76.7 0.6 multiply_reduce_fusion
  77.3 1.9 divide_convert_fusion
  79.2 1.1 copy-done.2
  80.3 1.6 fusion.20
  81.9 2.6 %copy.92 = f32[16,128,128]{2,1,0:T(8,128)} copy(f32[16,128,128]{1,2,0:T(8,128)} %fusion.20) | data formatting | bytes 2097152 | tf_op jit(solution)/shard_map/thd,the->hde/dot_general | solution.py:97
  84.5 1.4 transpose_reshape_reshape.3
  85.9 0.9 dynamic-slice_bitcast_fusion
  86.9 1.2 collective-permute-start.1
  88.0 2.1 %collective-permute-start.2 = (f32[1,16384]{1,0:T(1,128)S(1)}, f32[1,16384]{1,0:T(1,128)S(1)}, u32[]{:S(2)}, u32[]{:S(2)}) collective-permute-start(f32[1,16384]{1,0:T(1,128)S(1)} %get-tuple-element.34), channel_id=1, source_target_pairs={{0,3},{1,4},{2,5},{3,6},{4,7},{5,8},{6,9},{7,10},{8,11},{9,12},{10... | collective-permute-start | bytes 196616 | tf_op jit(solution)/shard_map/ppermute | solution.py:56
  90.1 0.8 collective-permute-start.3
  91.0 2.4 %collective-permute-done = f32[1,16384]{1,0:T(1,128)S(1)} collective-permute-done((f32[1,16384]{1,0:T(1,128)S(1)}, f32[1,16384]{1,0:T(1,128)S(1)}, u32[]{:S(2)}, u32[]{:S(2)}) %collective-permute-start) | collective-permute-done | bytes 65568 | tf_op jit(solution)/shard_map/ppermute | solution.py:56
  93.9 0.6 collective-permute-done.1
  94.5 1.7 collective-permute-start.6
  96.2 1.8 collective-permute-start.7
  98.0 0.8 collective-permute-start.8
  98.7 6.3 %collective-permute-done.4 = f32[1,16384]{1,0:T(1,128)S(1)} collective-permute-done((f32[1,16384]{1,0:T(1,128)S(1)}, f32[1,16384]{1,0:T(1,128)S(1)}, u32[]{:S(2)}, u32[]{:S(2)}) %collective-permute-start.4) | collective-permute-done | bytes 65568 | tf_op jit(solution)/shard_map/ppermute | solution.py:56
  105.3 1.4 collective-permute-start.10
  106.7 2.9 %collective-permute-start.11 = (f32[1,16384]{1,0:T(1,128)S(1)}, f32[1,16384]{1,0:T(1,128)S(1)}, u32[]{:S(2)}, u32[]{:S(2)}) collective-permute-start(f32[1,16384]{1,0:T(1,128)S(1)} %get-tuple-element.25), channel_id=1, source_target_pairs={{0,12},{1,13},{2,14},{3,15},{4,0},{5,1},{6,2},{7,3},{8,4},{9,5},{1... | collective-permute-start | bytes 196616 | tf_op jit(solution)/shard_map/ppermute | solution.py:56
  109.6 1.5 collective-permute-start.12
  111.1 2.5 %collective-permute-start.13 = (f32[1,16384]{1,0:T(1,128)S(1)}, f32[1,16384]{1,0:T(1,128)S(1)}, u32[]{:S(2)}, u32[]{:S(2)}) collective-permute-start(f32[1,16384]{1,0:T(1,128)S(1)} %get-tuple-element.23), channel_id=1, source_target_pairs={{0,14},{1,15},{2,0},{3,1},{4,2},{5,3},{6,4},{7,5},{8,6},{9,7},{10,... | collective-permute-start | bytes 196616 | tf_op jit(solution)/shard_map/ppermute | solution.py:56
  113.7 0.6 pad_clamp_fusion
  114.4 1.7 collective-permute-done.13
  116.1 0.8 collective-permute-done.14
  116.9 0.6 copy-done.22
  117.5 3.2 %stack.63 = f32[16,1,16384]{2,0,1:T(8,128)S(1)} concatenate(f32[1,1,16384]{2,0,1:T(1,128)S(1)} %get-tuple-element.37, f32[1,1,16384]{2,0,1:T(1,128)S(1)} %bitcast.184, f32[1,1,16384]{2,0,1:T(1,128)S(1)} %bitcast.185, f32[1,1,16384]{2,0,1:T(1,128)S(1)} %bitcast.186, f32[1,1,16384]{2,0,1:T(1,128)S(1)} %bitcast.187, f32[1,1,16384]{2,0,1:T(1,128)S(1)} %bitcast.188, ...), dimensions={0} | concatenate | bytes 2097152 | tf_op jit(solution)/shard_map/stack | solution.py:58
  120.7 1.9 %gather_fusion = f32[16,16384]{1,0:T(8,128)} fusion(f32[16,16384]{1,0:T(8,128)S(1)} %bitcast.170, s32[1024]{0:T(1024)} %pad_clamp_fusion), kind=kCustom, calls=%fused_computation | custom fusion | bytes 2097216 | tf_op jit(solution)/shard_map/gather | solution.py:59
  122.6 1.8 fusion.1
  124.4 1.0 reduce.3
  125.8 20.4 %all_to_all.61 = bf16[16,2,8192]{2,1,0:T(2,128)(2,1)} all-to-all(bf16[16,2,8192]{2,1,0:T(2,128)(2,1)S(1)} %reshape.164), channel_id=1, replica_groups=mesh['groups'=2,'seq'=16] {'seq'}, dimensions={0} | all-to-all | bytes 1048576 | tf_op jit(solution)/shard_map/all_to_all | solution.py:62
  146.2 4.5 %all-to-all-start.2 = ((bf16[16,384,128]{1,2,0:T(8,128)(2,1)}), bf16[16,384,128]{1,2,0:T(8,128)(2,1)}, u32[]{:S(2)}, u32[]{:S(2)}) async-start(bf16[16,384,128]{1,2,0:T(8,128)(2,1)} %get-tuple-element.21), calls=%async_computation.2 | async-start | bytes 3145728 | tf_op jit(solution)/shard_map/all_to_all | solution.py:93
  150.7 1.6 fusion.35
  152.4 1.7 select_convert_fusion
  154.1 2.7 %fusion.3 = bf16[384,16,128]{0,2,1:T(8,128)(2,1)} fusion(f32[16,128,384]{2,1,0:T(8,128)S(1)} %fusion.35, bf16[16,384,384]{2,1,0:T(8,128)(2,1)S(1)} %select_convert_fusion, bf16[384,16,128]{0,2,1:T(8,128)(2,1)S(1)} %copy-done.7), kind=kOutput, calls=%fused_computation.10 | convolution fusion | flops 605552640 | bytes 11010048 | tf_op jit(solution)/shard_map/hts,shd->thd/dot_general | solution.py:101
  156.8 2.6 %copy.97 = bf16[384,2048]{1,0:T(8,128)(2,1)} copy(bf16[384,2048]{0,1:T(8,128)(2,1)} %bitcast.173) | data formatting | bytes 3145728
  159.4 5.2 %fusion.36 = f32[16,128,384]{2,1,0:T(8,128)} fusion(bf16[384,16,128]{0,2,1:T(8,128)(2,1)S(1)} %copy-done.3, bf16[16,384,384]{2,1,0:T(8,128)(2,1)} %select_convert_fusion.1), kind=kOutput, calls=%fused_computation.74 | convolution fusion | flops 603979776 | bytes 9437184 | tf_op jit(solution)/shard_map/hts,the->she/dot_general | solution.py:107
  164.6 3.5 %reshape.165 = bf16[16,1,16384]{2,1,0:T(2,128)(2,1)} reshape(bf16[16,2,8192]{2,1,0:T(2,128)(2,1)} %all_to_all.61) | data formatting | bytes 1048576
  168.0 5.2 %reduce.1 = bf16[16,16384]{1,0:T(8,128)(2,1)} reduce(bf16[16,1,16384]{2,1,0:T(2,128)(2,1)} %reshape.165, bf16[]{:T(256)} %constant.121), dimensions={1}, to_apply=%all_to_all.54.reduce_sub_computation | reduce | bytes 1048578 | tf_op jit(solution)/shard_map/all_to_all | solution.py:62
  173.2 1.1 copy.110
  174.4 4.0 %add_convert_fusion = bf16[16,128,384]{2,1,0:T(8,128)(2,1)} fusion(f32[16,128,384]{2,1,0:T(8,128)} %fusion.36, bf16[16,128,128]{2,1,0:T(8,128)(2,1)S(1)} %bitcast.178, bf16[384,2048]{1,0:T(8,128)(2,1)S(1)} %copy-done.10), kind=kOutput, calls=%fused_computation.12 | convolution fusion | flops 202899456 | bytes 6815744 | tf_op jit(solution)/shard_map/shd,hde->she/dot_general | solution.py:108
  178.4 2.6 %copy.99 = bf16[384,2048]{1,0:T(8,128)(2,1)} copy(bf16[384,2048]{0,1:T(8,128)(2,1)} %bitcast.175) | data formatting | bytes 3145728
  181.1 0.8 fusion.5
  181.8 0.6 copy-done.9
  182.5 3.7 %fusion.2 = bf16[384,16,128]{0,2,1:T(8,128)(2,1)S(1)} fusion(f32[16,128,384]{2,1,0:T(8,128)S(1)} %fusion.5, bf16[16,384,384]{2,1,0:T(8,128)(2,1)} %copy-done.5, bf16[384,2048]{1,0:T(8,128)(2,1)S(1)} %copy-done.9), kind=kOutput, calls=%fused_computation.8 | convolution fusion | flops 605552640 | bytes 11010048 | tf_op jit(solution)/shard_map/hts,thd->shd/dot_general | solution.py:105
  186.2 1.6 copy.98
  187.8 2.6 %copy.84 = bf16[16,384,128]{2,1,0:T(8,128)(2,1)} copy(bf16[16,384,128]{1,2,0:T(8,128)(2,1)} %all-to-all-done.2) | data formatting | bytes 3145728 | tf_op jit(solution)/shard_map/all_to_all | solution.py:93
  (62 shorter events, 1.9 us)
Async XLA Ops:
  0.6 5.2 %copy-start = (bf16[384,2048]{1,0:T(8,128)(2,1)S(1)}, bf16[384,2048]{1,0:T(8,128)(2,1)}, u32[]{:S(2)}) copy-start(bf16[384,2048]{1,0:T(8,128)(2,1)} %param.6) | copy-start | bytes 4718596
  5.9 1.1 copy-start.6
  43.0 19.6 %all-to-all-start.1 = ((bf16[16,2,8192]{2,1,0:T(2,128)(2,1)}), bf16[16,2,8192]{2,1,0:T(2,128)(2,1)}, u32[]{:S(2)}, u32[]{:S(2)}) async-start(bf16[16,2,8192]{2,1,0:T(2,128)(2,1)} %reshape.162), calls=%async_computation.1 | async-start | bytes 1048576 | tf_op jit(solution)/shard_map/all_to_all | solution.py:41
  48.3 3.2 %copy-start.8 = (bf16[384,2048]{1,0:T(8,128)(2,1)S(1)}, bf16[384,2048]{1,0:T(8,128)(2,1)}, u32[]{:S(2)}) copy-start(bf16[384,2048]{1,0:T(8,128)(2,1)} %param.4) | copy-start | bytes 4718596
  72.3 0.9 copy-start.11
  72.3 2.5 %copy-start.4 = (bf16[16,384,384]{2,1,0:T(8,128)(2,1)S(1)}, bf16[16,384,384]{2,1,0:T(8,128)(2,1)}, u32[]{:S(2)}) copy-start(bf16[16,384,384]{2,1,0:T(8,128)(2,1)} %select_convert_fusion.1) | copy-start | bytes 14155780
  74.8 1.9 copy-start.1
  79.2 1.1 copy-start.2
  86.8 6.6 %collective-permute-start = (f32[1,16384]{1,0:T(1,128)S(1)}, f32[1,16384]{1,0:T(1,128)S(1)}, u32[]{:S(2)}, u32[]{:S(2)}) collective-permute-start(f32[1,16384]{1,0:T(1,128)S(1)} %get-tuple-element.36), channel_id=1, source_target_pairs={{0,1},{1,2},{2,3},{3,4},{4,5},{5,6},{6,7},{7,8},{8,9},{9,10},{10,1... | collective-permute-start | bytes 196616 | tf_op jit(solution)/shard_map/ppermute | solution.py:56
  86.9 7.7 %collective-permute-start.1 = (f32[1,16384]{1,0:T(1,128)S(1)}, f32[1,16384]{1,0:T(1,128)S(1)}, u32[]{:S(2)}, u32[]{:S(2)}) collective-permute-start(f32[1,16384]{1,0:T(1,128)S(1)} %get-tuple-element.35), channel_id=1, source_target_pairs={{0,2},{1,3},{2,4},{3,5},{4,6},{5,7},{6,8},{7,9},{8,10},{9,11},{10,... | collective-permute-start | bytes 196616 | tf_op jit(solution)/shard_map/ppermute | solution.py:56
  88.0 8.2 %collective-permute-start.2 = (f32[1,16384]{1,0:T(1,128)S(1)}, f32[1,16384]{1,0:T(1,128)S(1)}, u32[]{:S(2)}, u32[]{:S(2)}) collective-permute-start(f32[1,16384]{1,0:T(1,128)S(1)} %get-tuple-element.34), channel_id=1, source_target_pairs={{0,3},{1,4},{2,5},{3,6},{4,7},{5,8},{6,9},{7,10},{8,11},{9,12},{10... | collective-permute-start | bytes 196616 | tf_op jit(solution)/shard_map/ppermute | solution.py:56
  90.1 7.9 %collective-permute-start.3 = (f32[1,16384]{1,0:T(1,128)S(1)}, f32[1,16384]{1,0:T(1,128)S(1)}, u32[]{:S(2)}, u32[]{:S(2)}) collective-permute-start(f32[1,16384]{1,0:T(1,128)S(1)} %get-tuple-element.33), channel_id=1, source_target_pairs={{0,4},{1,5},{2,6},{3,7},{4,8},{5,9},{6,10},{7,11},{8,12},{9,13},{1... | collective-permute-start | bytes 196616 | tf_op jit(solution)/shard_map/ppermute | solution.py:56
  90.9 14.2 %collective-permute-start.4 = (f32[1,16384]{1,0:T(1,128)S(1)}, f32[1,16384]{1,0:T(1,128)S(1)}, u32[]{:S(2)}, u32[]{:S(2)}) collective-permute-start(f32[1,16384]{1,0:T(1,128)S(1)} %get-tuple-element.32), channel_id=1, source_target_pairs={{0,5},{1,6},{2,7},{3,8},{4,9},{5,10},{6,11},{7,12},{8,13},{9,14},{... | collective-permute-start | bytes 196616 | tf_op jit(solution)/shard_map/ppermute | solution.py:56
  93.3 11.9 %collective-permute-start.5 = (f32[1,16384]{1,0:T(1,128)S(1)}, f32[1,16384]{1,0:T(1,128)S(1)}, u32[]{:S(2)}, u32[]{:S(2)}) collective-permute-start(f32[1,16384]{1,0:T(1,128)S(1)} %get-tuple-element.31), channel_id=1, source_target_pairs={{0,6},{1,7},{2,8},{3,9},{4,10},{5,11},{6,12},{7,13},{8,14},{9,15},... | collective-permute-start | bytes 196616 | tf_op jit(solution)/shard_map/ppermute | solution.py:56
  94.5 12.2 %collective-permute-start.6 = (f32[1,16384]{1,0:T(1,128)S(1)}, f32[1,16384]{1,0:T(1,128)S(1)}, u32[]{:S(2)}, u32[]{:S(2)}) collective-permute-start(f32[1,16384]{1,0:T(1,128)S(1)} %get-tuple-element.30), channel_id=1, source_target_pairs={{0,7},{1,8},{2,9},{3,10},{4,11},{5,12},{6,13},{7,14},{8,15},{9,0},... | collective-permute-start | bytes 196616 | tf_op jit(solution)/shard_map/ppermute | solution.py:56
  96.2 13.4 %collective-permute-start.7 = (f32[1,16384]{1,0:T(1,128)S(1)}, f32[1,16384]{1,0:T(1,128)S(1)}, u32[]{:S(2)}, u32[]{:S(2)}) collective-permute-start(f32[1,16384]{1,0:T(1,128)S(1)} %get-tuple-element.29), channel_id=1, source_target_pairs={{0,8},{1,9},{2,10},{3,11},{4,12},{5,13},{6,14},{7,15},{8,0},{9,1},... | collective-permute-start | bytes 196616 | tf_op jit(solution)/shard_map/ppermute | solution.py:56
  98.0 13.1 %collective-permute-start.8 = (f32[1,16384]{1,0:T(1,128)S(1)}, f32[1,16384]{1,0:T(1,128)S(1)}, u32[]{:S(2)}, u32[]{:S(2)}) collective-permute-start(f32[1,16384]{1,0:T(1,128)S(1)} %get-tuple-element.28), channel_id=1, source_target_pairs={{0,9},{1,10},{2,11},{3,12},{4,13},{5,14},{6,15},{7,0},{8,1},{9,2},... | collective-permute-start | bytes 196616 | tf_op jit(solution)/shard_map/ppermute | solution.py:56
  105.1 8.6 %collective-permute-start.9 = (f32[1,16384]{1,0:T(1,128)S(1)}, f32[1,16384]{1,0:T(1,128)S(1)}, u32[]{:S(2)}, u32[]{:S(2)}) collective-permute-start(f32[1,16384]{1,0:T(1,128)S(1)} %get-tuple-element.27), channel_id=1, source_target_pairs={{0,10},{1,11},{2,12},{3,13},{4,14},{5,15},{6,0},{7,1},{8,2},{9,3},... | collective-permute-start | bytes 196616 | tf_op jit(solution)/shard_map/ppermute | solution.py:56
  105.3 9.1 %collective-permute-start.10 = (f32[1,16384]{1,0:T(1,128)S(1)}, f32[1,16384]{1,0:T(1,128)S(1)}, u32[]{:S(2)}, u32[]{:S(2)}) collective-permute-start(f32[1,16384]{1,0:T(1,128)S(1)} %get-tuple-element.26), channel_id=1, source_target_pairs={{0,11},{1,12},{2,13},{3,14},{4,15},{5,0},{6,1},{7,2},{8,3},{9,4},{... | collective-permute-start | bytes 196616 | tf_op jit(solution)/shard_map/ppermute | solution.py:56
  106.7 10.2 %copy-start.14 = (f32[1,16384]{1,0:T(1,128)}, f32[1,16384]{1,0:T(1,128)S(1)}, u32[]{:S(2)}) copy-start(f32[1,16384]{1,0:T(1,128)S(1)} %collective-permute-done.6) | copy-start | bytes 196612
  106.7 7.6 %collective-permute-start.11 = (f32[1,16384]{1,0:T(1,128)S(1)}, f32[1,16384]{1,0:T(1,128)S(1)}, u32[]{:S(2)}, u32[]{:S(2)}) collective-permute-start(f32[1,16384]{1,0:T(1,128)S(1)} %get-tuple-element.25), channel_id=1, source_target_pairs={{0,12},{1,13},{2,14},{3,15},{4,0},{5,1},{6,2},{7,3},{8,4},{9,5},{1... | collective-permute-start | bytes 196616 | tf_op jit(solution)/shard_map/ppermute | solution.py:56
  109.6 7.3 %copy-start.15 = (f32[1,16384]{1,0:T(1,128)}, f32[1,16384]{1,0:T(1,128)S(1)}, u32[]{:S(2)}) copy-start(f32[1,16384]{1,0:T(1,128)S(1)} %collective-permute-done.7) | copy-start | bytes 196612
  109.6 4.8 %collective-permute-start.12 = (f32[1,16384]{1,0:T(1,128)S(1)}, f32[1,16384]{1,0:T(1,128)S(1)}, u32[]{:S(2)}, u32[]{:S(2)}) collective-permute-start(f32[1,16384]{1,0:T(1,128)S(1)} %get-tuple-element.24), channel_id=1, source_target_pairs={{0,13},{1,14},{2,15},{3,0},{4,1},{5,2},{6,3},{7,4},{8,5},{9,6},{10... | collective-permute-start | bytes 196616 | tf_op jit(solution)/shard_map/ppermute | solution.py:56
  111.1 5.8 %copy-start.16 = (f32[1,16384]{1,0:T(1,128)}, f32[1,16384]{1,0:T(1,128)S(1)}, u32[]{:S(2)}) copy-start(f32[1,16384]{1,0:T(1,128)S(1)} %collective-permute-done.8) | copy-start | bytes 196612
  111.1 4.9 %collective-permute-start.13 = (f32[1,16384]{1,0:T(1,128)S(1)}, f32[1,16384]{1,0:T(1,128)S(1)}, u32[]{:S(2)}, u32[]{:S(2)}) collective-permute-start(f32[1,16384]{1,0:T(1,128)S(1)} %get-tuple-element.23), channel_id=1, source_target_pairs={{0,14},{1,15},{2,0},{3,1},{4,2},{5,3},{6,4},{7,5},{8,6},{9,7},{10,... | collective-permute-start | bytes 196616 | tf_op jit(solution)/shard_map/ppermute | solution.py:56
  113.6 3.3 %copy-start.17 = (f32[1,16384]{1,0:T(1,128)}, f32[1,16384]{1,0:T(1,128)S(1)}, u32[]{:S(2)}) copy-start(f32[1,16384]{1,0:T(1,128)S(1)} %collective-permute-done.9) | copy-start | bytes 196612
  113.6 3.2 %collective-permute-start.14 = (f32[1,16384]{1,0:T(1,128)S(1)}, f32[1,16384]{1,0:T(1,128)S(1)}, u32[]{:S(2)}, u32[]{:S(2)}) collective-permute-start(f32[1,16384]{1,0:T(1,128)S(1)} %get-tuple-element.22), channel_id=1, source_target_pairs={{0,15},{1,0},{2,1},{3,2},{4,3},{5,4},{6,5},{7,6},{8,7},{9,8},{10,9... | collective-permute-start | bytes 196616 | tf_op jit(solution)/shard_map/ppermute | solution.py:56
  114.3 2.5 %copy-start.18 = (f32[1,16384]{1,0:T(1,128)}, f32[1,16384]{1,0:T(1,128)S(1)}, u32[]{:S(2)}) copy-start(f32[1,16384]{1,0:T(1,128)S(1)} %collective-permute-done.10) | copy-start | bytes 196612
  114.3 2.5 %copy-start.19 = (f32[1,16384]{1,0:T(1,128)}, f32[1,16384]{1,0:T(1,128)S(1)}, u32[]{:S(2)}) copy-start(f32[1,16384]{1,0:T(1,128)S(1)} %collective-permute-done.11) | copy-start | bytes 196612
  114.4 2.5 %copy-start.20 = (f32[1,16384]{1,0:T(1,128)}, f32[1,16384]{1,0:T(1,128)S(1)}, u32[]{:S(2)}) copy-start(f32[1,16384]{1,0:T(1,128)S(1)} %collective-permute-done.12) | copy-start | bytes 196612
  116.0 0.9 copy-start.21
  116.9 0.6 copy-start.22
  146.2 4.6 %copy-start.3 = (bf16[384,16,128]{0,2,1:T(8,128)(2,1)S(1)}, bf16[384,16,128]{0,2,1:T(8,128)(2,1)}, u32[]{:S(2)}) copy-start(bf16[384,16,128]{0,2,1:T(8,128)(2,1)} %copy-done.2) | copy-start | bytes 4718596
  146.2 41.6 %all-to-all-start.2 = ((bf16[16,384,128]{1,2,0:T(8,128)(2,1)}), bf16[16,384,128]{1,2,0:T(8,128)(2,1)}, u32[]{:S(2)}, u32[]{:S(2)}) async-start(bf16[16,384,128]{1,2,0:T(8,128)(2,1)} %get-tuple-element.21), calls=%async_computation.2 | async-start | bytes 3145728 | tf_op jit(solution)/shard_map/all_to_all | solution.py:93
  152.3 1.7 copy-start.7
  154.1 2.7 %copy-start.5 = (bf16[16,384,384]{2,1,0:T(8,128)(2,1)}, bf16[16,384,384]{2,1,0:T(8,128)(2,1)S(1)}, u32[]{:S(2)}) copy-start(bf16[16,384,384]{2,1,0:T(8,128)(2,1)S(1)} %select_convert_fusion) | copy-start | bytes 14155780
  168.0 6.3 %copy-start.10 = (bf16[384,2048]{1,0:T(8,128)(2,1)S(1)}, bf16[384,2048]{1,0:T(8,128)(2,1)}, u32[]{:S(2)}) copy-start(bf16[384,2048]{1,0:T(8,128)(2,1)} %param.5) | copy-start | bytes 4718596
  174.4 4.1 %copy-start.12 = (bf16[2,8,128,128]{3,2,1,0:T(8,128)(2,1)}, bf16[2,8,128,128]{3,2,1,0:T(8,128)(2,1)S(1)}, u32[]{:S(2)}) copy-start(bf16[2,8,128,128]{3,2,1,0:T(8,128)(2,1)S(1)} %copy.110) | copy-start | bytes 1572868
  178.4 2.6 %copy-start.13 = (bf16[2,8,128,128]{3,2,1,0:T(8,128)(2,1)S(1)}, bf16[2,8,128,128]{3,2,1,0:T(8,128)(2,1)}, u32[]{:S(2)}) copy-start(bf16[2,8,128,128]{3,2,1,0:T(8,128)(2,1)} %copy-done.12) | copy-start | bytes 1572868
  181.1 1.4 copy-start.9
